TPU v7x, 256 devices: a whole 4x4x8 slice. The times are simulated.
256 devices in a mesh: dom: 16 (over y_hi, x, core), orient: 16 (over z, y_lo).
Axes of the slice: x: 4, y: 4 (y_hi: 2, y_lo: 2; y = y_hi * 2 + y_lo), z: 8, core: 2. Of those that a mesh axis runs over, the one named last changes fastest.
Arguments:
- images: bfloat16 [2816, 32768], P('dom'), may hold values from -128 to 128
- ctf_table: bfloat16 [8, 32768], replicated, may hold values from 0.29882812 to 1.5
- group_ids: int32 [2816], P('dom'), may hold values from 0 to 7
- projections: bfloat16 [2048, 32768], P('orient', 'dom'), may hold values from -4 to 4
- log_prior: float32 [2048], P('orient'), may hold values from -2 to 3
Outputs:
- numerator: bfloat16 [32768, 2048], P('dom', 'orient')
All inputs are finite; a program needn't handle non-finite values.
Results may differ from a plain program's by a relative error of at most 0.017.
Values may be sent and summed in bfloat16 or wider, within the bound.
A program may use at most 128 MiB of HBM per device.

v0:
```python
import jax
import jax.numpy as jnp
from jax import lax
from jax.sharding import PartitionSpec as P


def body(images, ctf_table, group_ids, projections, log_prior):
    highest = lax.Precision.HIGHEST
    groups_count = ctf_table.shape[0]
    onehot = (group_ids[:, None] == jnp.arange(groups_count, dtype=jnp.int32)[None, :]).astype(
        jnp.float32
    )
    ctf_wide = ctf_table.astype(jnp.float32)
    ctf_rows = jnp.dot(onehot, ctf_wide, precision=highest)
    weighted = (ctf_rows * images.astype(jnp.float32)).astype(jnp.bfloat16)
    ctf_square = ctf_wide * ctf_wide
    piece = lax.all_gather(projections, "dom", axis=1, tiled=True)
    columns = weighted
    dots_acc = lax.dot_general(
        columns, piece, (((1,), (1,)), ((), ())), preferred_element_type=jnp.float32
    )
    piece_sq = piece.astype(jnp.float32) ** 2
    norms_acc = lax.dot_general(ctf_square, piece_sq, (((1,), (1,)), ((), ())), precision=highest)
    lookup = jnp.dot(onehot, norms_acc, precision=highest)
    scores = (dots_acc - 0.5 * lookup) * (1.0 / jnp.sqrt(jnp.float32(images.shape[1]))) + log_prior[
        None, :
    ]
    top = lax.pmax(jnp.max(scores, axis=1), "orient")
    expo = jnp.exp(scores - top[:, None])
    total = lax.psum(jnp.sum(expo, axis=1), "orient")
    weights = (expo / total[:, None]).astype(jnp.bfloat16)
    columns = weighted
    term = lax.dot_general(
        columns, weights, (((0,), (0,)), ((), ())), preferred_element_type=jnp.float32
    )
    rounded = lax.optimization_barrier(term.astype(jnp.bfloat16))
    return lax.psum_scatter(
        rounded.astype(jnp.float32).astype(jnp.bfloat16), "dom", scatter_dimension=0, tiled=True
    )


def solution(mesh):
    placed = (P("dom", None), P(), P("dom"), P("orient", "dom"), P("orient"))
    return jax.shard_map(
        body, mesh=mesh, in_specs=placed, out_specs=P("dom", "orient"), check_vma=False
    )
```

profile of v0, /device:TPU:1, one launch (start us, length us, event | category | flops | bytes accessed | tf_op | source)
XLA Modules:
  0.0 307.1 jit_solution(6543194802870145686)
XLA Ops:
  6.5 0.0 all-gather.2.cloned.1.call-start
  6.5 0.7 all-gather.2.cloned.1.call-update
  7.3 0.0 copy-start
  7.3 0.0 reduce-scatter.2.cloned.1.call-start
  7.3 10.3 %fusion = bf16[176,32768]{1,0:T(8,128)(2,1)} fusion(bf16[8,32768]{1,0:T(8,128)(2,1)} %param.6, bf16[176,32768]{1,0:T(8,128)(2,1)} %param.5, s32[176]{0:T(256)} %param.7), kind=kOutput, calls=%fused_computation.1 | convolution fusion | flops 109577600 | bytes 23593664 | tf_op jit(solution)/shard_map/dot_general | solution.py:14
  17.6 74.6 %all-gather.2.cloned.1.call-done = bf16[128,32768]{1,0:T(8,128)(2,1)} async-done(((bf16[128,2048]{1,0:T(8,128)(2,1)}), bf16[128,32768]{1,0:T(8,128)(2,1)}) %all-gather.2.cloned.1.call-update) | async-done | bytes 8388624 | tf_op jit(solution)/shard_map/all_gather | solution.py:17
  92.2 0.0 copy-done
  92.2 15.4 %fusion.1 = f32[8,128]{1,0:T(8,128)S(1)} fusion(bf16[128,32768]{1,0:T(8,128)(2,1)} %all-gather.2.cloned.1.call-done, bf16[8,32768]{1,0:T(8,128)(2,1)S(1)} %copy-done), kind=kOutput, calls=%fused_computation.3 | convolution fusion | flops 411566080 | bytes 8916992 | tf_op jit(solution)/shard_map/dot_general | solution.py:23
  107.6 0.0 copy-start.1
  107.6 0.0 copy-start.2
  107.6 9.8 %fusion.15 = f32[176,128]{1,0:T(8,128)S(1)} fusion(bf16[176,32768]{1,0:T(8,128)(2,1)} %fusion, bf16[128,32768]{1,0:T(8,128)(2,1)} %all-gather.2.cloned.1.call-done), kind=kOutput, calls=%fused_computation.21 | convolution fusion | flops 1476395008 | bytes 20013056 | tf_op jit(solution)/shard_map/dot_general | solution.py:19
  117.4 0.0 copy-done.1
  117.4 0.0 copy-done.2
  117.4 0.3 fusion.14
  117.8 26.9 %pmax.7 = f32[176]{0:T(256)S(1)} all-reduce(f32[176]{0:T(256)S(1)} %get-tuple-element.5), channel_id=1, replica_groups=mesh['dom'=16,'orient'=16] {'orient'}, use_global_device_ids=true, to_apply=%region_1.0 | all-reduce | flops 176 | bytes 1408 | tf_op jit(solution)/shard_map/pmax | solution.py:28
  144.7 0.2 fusion.9
  144.9 23.9 %psum.7 = f32[176]{0:T(256)S(1)} all-reduce(f32[176]{0:T(256)S(1)} %fusion.9), channel_id=1, replica_groups=mesh['dom'=16,'orient'=16] {'orient'}, use_global_device_ids=true, to_apply=%region_3.0 | all-reduce | flops 176 | bytes 1408 | tf_op jit(solution)/shard_map/psum | solution.py:30
  168.8 12.3 %convolution_convert_fusion = bf16[32768,128]{1,0:T(8,128)(2,1)} fusion(bf16[176,32768]{1,0:T(8,128)(2,1)} %fusion, f32[176,128]{1,0:T(8,128)S(1)} %get-tuple-element.6, f32[176]{0:T(256)S(1)} %psum.7, f32[176]{0:T(256)S(1)} %pmax.7), kind=kOutput, calls=%fused_computation.2 | convolution fusion | flops 1480656896 | bytes 20014464 | tf_op jit(solution)/shard_map/dot_general | solution.py:33
  181.0 0.0 reduce-scatter.2.cloned.1.call-update
  181.0 119.3 %reduce-scatter.2.cloned.1.call-done = bf16[2048,128]{1,0:T(8,128)(2,1)} async-done(((bf16[32768,128]{1,0:T(8,128)(2,1)}), bf16[2048,128]{1,0:T(8,128)(2,1)}) %reduce-scatter.2.cloned.1.call-update) | async-done | bytes 524304 | tf_op jit(solution)/shard_map/reduce_scatter | solution.py:37
Async XLA Ops:
  6.5 85.7 %all-gather.2.cloned.1.call-start = ((), (), s32[]{:S(2)}) async-start(), calls=%async_computation.1 | async-start | bytes 8912896 | tf_op jit(solution)/shard_map/all_gather | solution.py:17
  7.3 85.0 %copy-start = (bf16[8,32768]{1,0:T(8,128)(2,1)S(1)}, bf16[8,32768]{1,0:T(8,128)(2,1)}, u32[]{:S(2)}) copy-start(bf16[8,32768]{1,0:T(8,128)(2,1)} %param.6) | copy-start | bytes 1572868
  7.3 293.0 %reduce-scatter.2.cloned.1.call-start = ((), (), s32[]{:S(2)}) async-start(), calls=%async_computation.2 | async-start | bytes 8912896 | tf_op jit(solution)/shard_map/reduce_scatter | solution.py:37
  107.6 9.9 %copy-start.1 = (s32[176]{0:T(256)S(1)}, s32[176]{0:T(256)}, u32[]{:S(2)}) copy-start(s32[176]{0:T(256)} %param.7) | copy-start | bytes 2116
  107.6 9.9 %copy-start.2 = (f32[128]{0:T(128)S(1)}, f32[128]{0:T(128)}, u32[]{:S(2)}) copy-start(f32[128]{0:T(128)} %param.9) | copy-start | bytes 1540
Sparse Core Ops, SparseCore 0:
  10.1 82.0 all-gather.1
  181.2 119.0 reduce-scatter.1
where the time goes:
time: 307 us
  waiting for transfers between devices  195 us (64%)
  blocking collectives  50.8 us (17%)
  matrix products  48.1 us (16%)
  between operations  13.4 us (4%)
    reduce_scatter x1, waiting for transfers between devices, body(): lax.psum_scatter(rounded.astype(jnp.float32).astype(jnp.bfloat16), 'dom',...  119 us
    all_gather x1, waiting for transfers between devices, body(): piece = lax.all_gather(projections, 'dom', axis=1, tiled=True)  74.6 us
    pmax x1, blocking collectives, body(): top = lax.pmax(jnp.max(scores, axis=1), 'orient')  26.9 us
    psum x1, blocking collectives, body(): total = lax.psum(jnp.sum(expo, axis=1), 'orient')  23.9 us
    dot_general x1, matrix products, body(): lax.dot_general(ctf_square, piece_sq, (((1,), (1,)), ((), ())), precision...  15.4 us
    dot_general x1, matrix products, body(): lax.dot_general(columns, weights, (((0,), (0,)), ((), ())), preferred_ele...  12.3 us
    dot_general x1, matrix products, body(): ctf_rows = jnp.dot(onehot, ctf_wide, precision=highest)  10.3 us
    dot_general x1, matrix products, body(): lax.dot_general(columns, piece, (((1,), (1,)), ((), ())), preferred_eleme...  9.83 us
  transfers between devices with their start and end apart: 2, of which 2 were waited for; matrix products, arithmetic and copies ran while one was open for 3% of the time, Pallas kernels for 0%

commit v1 on v0

v1 whole, which is shorter than its diff:
```python
import functools

import jax
import jax.numpy as jnp
import numpy as np
from jax import lax
from jax.experimental import pallas as pl
from jax.experimental.pallas import tpu as pltpu
from jax.sharding import PartitionSpec as P

BF = jnp.bfloat16
F32 = jnp.float32
MESH = pl.DeviceIdType.MESH
NX, NZ = 4, 8
NQ = 4
LOW, HIGH = (0, 1), (2, 3)
QS = (0, 1, 2, 3)
MIXED = (0, 2, 1, 3)
PAD = 256
ORDER = ((0, 0), (0, 3), (0, 1), (1, 0), (0, 2), (1, 2), (1, 3), (1, 1))
FAR, DIAG3, DIAG1, OWN3, OWN1, ACROSS, HALF = range(7)


def nt(a, b):
    return lax.dot_general(a, b, (((1,), (1,)), ((), ())), preferred_element_type=F32)


def nn(a, b):
    return jnp.dot(a, b, preferred_element_type=F32)


def split3(v):
    a = v.astype(BF)
    r = v - a.astype(F32)
    b = r.astype(BF)
    return a, b, (r - b.astype(F32)).astype(BF)


def kernel(
    images,
    ctf,
    gids,
    proj,
    prior,
    out,
    raw,
    weighted,
    stage,
    blocks,
    ctfv,
    ctf_sq,
    hot,
    hot_t,
    acc,
    norm,
    xsend,
    xrecv,
    stat,
    wts,
    part,
    rx,
    raw_sem,
    loc_sem,
    g_send,
    g_recv,
    w_send,
    w_recv,
    hot_sem,
    x_send,
    x_recv,
    st_send,
    st_recv,
    wt_send,
    wt_recv,
    r_send,
    r_recv,
):
    n_loc, pix = images.shape
    n_rows, width = proj.shape
    step = width // NQ
    scale = float(np.float32(1.0) / np.sqrt(np.float32(pix)))
    dom, ori = lax.axis_index("dom"), lax.axis_index("orient")
    yh, x, core = dom // (2 * NX), lax.rem(dom // 2, NX), lax.rem(dom, 2)
    z, yl = ori // 2, lax.rem(ori, 2)

    def device(yh_, x_, core_, yl_):
        return {"dom": (yh_ * NX + x_) * 2 + core_, "orient": z * 2 + yl_}

    xp = device(yh, lax.rem(x + 1, NX), core, yl)
    xm = device(yh, lax.rem(x + NX - 1, NX), core, yl)
    yp = device(1 - yh, x, core, 1 - yl)
    sib = device(yh, x, 1 - core, yl)
    near = device(yh, x, core, 1 - yl)
    diag = device(yh, x, 1 - core, 1 - yl)

    def peer(k):
        return {"dom": dom, "orient": lax.rem(ori + k, 2 * NZ)}

    def pixel_block(s, j, core_):
        yh_ = yh if s == 0 else 1 - yh
        return (yh_ * NX + lax.rem(x + j, NX)) * 2 + core_

    jobs = [(s, j, own) for s, j in ORDER for own in (0, 1)]
    n_raw = raw.shape[0]

    def raw_copy(i):
        s, j, own = jobs[i]
        d = pixel_block(s, j, core if own else 1 - core)
        start = pl.multiple_of(d * width, width)
        return pltpu.make_async_copy(
            images.at[:, pl.ds(start, width)], raw.at[i % n_raw], raw_sem.at[i % n_raw]
        )

    ctf_copy = pltpu.make_async_copy(ctf, ctfv, loc_sem.at[NQ])
    ctf_copy.start()
    for i in range(n_raw):
        raw_copy(i).start()
    own_copies = [
        pltpu.make_async_copy(
            proj.at[:, pl.ds(q * step, step)], blocks.at[0, 0, q], loc_sem.at[q]
        )
        for q in QS
    ]
    for copy in own_copies:
        copy.start()

    barrier = pltpu.get_barrier_semaphore()
    for who in (xp, xm, yp, sib, diag):
        pl.semaphore_signal(barrier, inc=1, device_id=who, device_id_type=MESH)

    @pl.loop(1, 2 * NZ)
    def _(k):
        pl.semaphore_signal(barrier, inc=1, device_id=peer(k), device_id_type=MESH)

    pl.semaphore_wait(barrier, 5 + 2 * NZ - 1)

    links = (xp, xm, yp)
    counts = [0, 0, 0]
    sent = []

    def gather(link, src, s, j, q):
        copy = pltpu.make_async_remote_copy(
            src_ref=src,
            dst_ref=blocks.at[s, j, q],
            send_sem=g_send.at[link, counts[link]],
            recv_sem=g_recv.at[s, j, q],
            device_id=links[link],
            device_id_type=MESH,
        )
        counts[link] += 1
        copy.start()
        sent.append(copy)

    def arrived(s, j, q):
        pltpu.make_async_remote_copy(
            src_ref=blocks.at[s, j, q],
            dst_ref=blocks.at[s, j, q],
            send_sem=g_send.at[0, 0],
            recv_sem=g_recv.at[s, j, q],
            device_id=xp,
            device_id_type=MESH,
        ).wait_recv()

    for a, b in zip(LOW + HIGH, HIGH + LOW):
        gather(0, proj.at[:, pl.ds(a * step, step)], 0, 3, a)
        gather(1, proj.at[:, pl.ds(b * step, step)], 0, 1, b)
        gather(2, proj.at[:, pl.ds(a * step, step)], 1, 0, a)

    group = lax.broadcasted_iota(jnp.int32, (n_rows, n_loc), 0)
    hot_full = jnp.where(group == gids[...], 1.0, 0.0)
    acc[0, 0] = jnp.zeros((n_rows, PAD), F32)
    acc[0, 0, :, :n_loc] = hot_full
    hot_t[...] = jnp.transpose(acc[0, 0])[:n_loc, :].astype(BF)
    twice = jnp.concatenate([acc[0, 0, :8, :], acc[0, 0, :8, :]], axis=0)
    hot[0] = twice.astype(BF)
    hot_copy = pltpu.make_async_remote_copy(
        src_ref=hot.at[0],
        dst_ref=hot.at[1],
        send_sem=hot_sem.at[0],
        recv_sem=hot_sem.at[1],
        device_id=sib,
        device_id_type=MESH,
    )
    hot_copy.start()
    acc[...] = jnp.zeros(acc.shape, F32)
    norm[...] = jnp.zeros(norm.shape, F32)
    ctf_copy.wait()

    def weigh(i):
        s, j, own = jobs[i]
        d = pixel_block(s, j, core if own else 1 - core)
        dst = weighted.at[0, s, j] if own else stage.at[s, j]
        raw_copy(i).wait()
        tile = 256

        @pl.loop(0, width // tile)
        def _(t):
            here = pl.ds(pl.multiple_of(t * tile, tile), tile)
            there = pl.ds(pl.multiple_of(d * width + t * tile, tile), tile)
            table = ctfv[:, there]
            rows = nn(hot_t[:, :8], table)
            dst[:, here] = (rows * raw[i % n_raw, :, here].astype(F32)).astype(BF)
            if own:
                wide = table.astype(F32)
                square = wide * wide
                high = square.astype(BF).astype(F32)
                both = jnp.concatenate([high, square - high], axis=0)
                ctf_sq[s, j, :, here] = both.astype(BF)

        if i + n_raw < len(jobs):
            raw_copy(i + n_raw).start()
        if not own:
            copy = weighted_copy(s, j)
            copy.start()

    def weighted_copy(s, j):
        return pltpu.make_async_remote_copy(
            src_ref=stage.at[s, j],
            dst_ref=weighted.at[1, s, j],
            send_sem=w_send.at[s, j],
            recv_sem=w_recv.at[s, j],
            device_id=sib,
            device_id_type=MESH,
        )

    def score(s, j, q):
        here = pl.ds(pl.multiple_of(q * step, step), step)
        block = blocks[s, j, q]
        for nb in (0, 1):
            acc[s, nb, :, :n_loc] += nt(block, weighted[nb, s, j, :, here])
        wide = block.astype(F32)
        square = wide * wide
        high = square.astype(BF)
        low = (square - high.astype(F32)).astype(BF)
        table = ctf_sq[s, j, :, here]
        norm[s] += nt(high, table) + nt(low, table)

    def score_block(s, j):
        @pl.loop(0, NQ)
        def _(q):
            score(s, j, q)

    for i in range(8):
        weigh(i)
    for a, b in zip(LOW, HIGH):
        arrived(0, 3, a)
        gather(0, blocks.at[0, 3, a], 0, 2, a)
        arrived(0, 1, b)
        gather(1, blocks.at[0, 1, b], 0, 2, b)
    for i in range(8, 16):
        weigh(i)
    for q in QS:
        arrived(1, 0, q)
        gather(0, blocks.at[1, 0, q], 1, 3, q)
        gather(1, blocks.at[1, 0, q], 1, 1, q)
    for copy in own_copies:
        copy.wait()
    weighted_copy(0, 0).wait_recv()
    score_block(0, 0)
    for a, b in zip(LOW, HIGH):
        arrived(0, 3, b)
        arrived(0, 1, a)
    weighted_copy(0, 3).wait_recv()
    score_block(0, 3)
    weighted_copy(0, 1).wait_recv()
    score_block(0, 1)
    for q in MIXED:
        arrived(0, 2, q)
        gather(2, blocks.at[0, 2, q], 1, 2, q)
    weighted_copy(0, 2).wait_recv()
    score_block(0, 2)

    hot_copy.wait()

    def partial_scores(s, nb):
        a, b, c = split3(norm[s])
        look = nn(a, hot[nb]) + nn(b, hot[nb]) + nn(c, hot[nb])
        return (acc[s, nb] - 0.5 * look) * scale

    def exchange(i, who):
        return pltpu.make_async_remote_copy(
            src_ref=xsend.at[i],
            dst_ref=xrecv.at[i],
            send_sem=x_send.at[i],
            recv_sem=x_recv.at[i],
            device_id=who,
            device_id_type=MESH,
        )

    prior_rows = jnp.transpose(jnp.broadcast_to(prior[...], (n_rows, n_rows)))[:, :1]
    xsend[0] = partial_scores(0, 0) + prior_rows
    xsend[1] = partial_scores(0, 1)
    exchange(0, near).start()
    exchange(1, diag).start()

    weighted_copy(1, 0).wait_recv()
    score_block(1, 0)
    for j in (2, 3, 1):
        weighted_copy(1, j).wait_recv()
    for a, q in zip(MIXED, QS):
        arrived(1, 2, a)
        score(1, 2, a)
        arrived(1, 3, q)
        score(1, 3, q)
        arrived(1, 1, q)
        score(1, 1, q)

    xsend[2] = partial_scores(1, 1)
    exchange(2, sib).start()
    mine = partial_scores(1, 0)
    exchange(0, near).wait_recv()
    exchange(1, diag).wait_recv()
    mine += xrecv[0] + xrecv[1]
    exchange(2, sib).wait_recv()
    scores = mine + xrecv[2]

    largest = jnp.max(scores, axis=0, keepdims=True)
    expo = jnp.exp(scores - largest)
    stat[0, 0:1] = largest
    stat[0, 1:2] = jnp.sum(expo, axis=0, keepdims=True)
    stat[0, 2:8] = jnp.zeros((6, PAD), F32)

    def stat_copy(k):
        return pltpu.make_async_remote_copy(
            src_ref=stat.at[0],
            dst_ref=stat.at[k],
            send_sem=st_send.at[k],
            recv_sem=st_recv.at[k],
            device_id=peer(k),
            device_id_type=MESH,
        )

    @pl.loop(1, 2 * NZ)
    def _(k):
        stat_copy(k).start()

    @pl.loop(1, 2 * NZ)
    def _(k):
        stat_copy(k).wait_recv()

    tops = stat[:, 0, :]
    top = jnp.max(tops, axis=0, keepdims=True)
    total = jnp.sum(stat[:, 1, :] * jnp.exp(tops - top), axis=0, keepdims=True)
    wts[1, 0] = (expo * (jnp.exp(largest - top) / total)).astype(BF)

    def weight_copy(i):
        s, nb, who = ((1, 1, sib), (0, 0, near), (0, 1, diag))[i]
        return pltpu.make_async_remote_copy(
            src_ref=wts.at[1, 0],
            dst_ref=wts.at[s, nb],
            send_sem=wt_send.at[i],
            recv_sem=wt_recv.at[i],
            device_id=who,
            device_id_type=MESH,
        )

    for i in range(3):
        weight_copy(i).start()

    counts2 = [0, 0, 0]

    def here(q):
        return pl.ds(q * step, step)

    def sums(s, j, q):
        return nn(wts[s, 0, :, :n_loc], weighted[0, s, j, :, here(q)]) + nn(
            wts[s, 1, :, :n_loc], weighted[1, s, j, :, here(q)]
        )

    def landed(kind, q):
        pltpu.make_async_remote_copy(
            src_ref=rx.at[kind, q],
            dst_ref=rx.at[kind, q],
            send_sem=r_send.at[0, 0],
            recv_sem=r_recv.at[kind, q],
            device_id=xp,
            device_id_type=MESH,
        ).wait_recv()
        return rx[kind, q].astype(F32)

    def scatter(link, kind, s, j, q, *added):
        for k in added:
            pass
        total_ = sums(s, j, q)
        for k in added:
            total_ = total_ + landed(k, q)
        part[s, j, q] = total_.astype(BF)
        copy = pltpu.make_async_remote_copy(
            src_ref=part.at[s, j, q],
            dst_ref=rx.at[kind, q],
            send_sem=r_send.at[link, counts2[link]],
            recv_sem=r_recv.at[kind, q],
            device_id=links[link],
            device_id_type=MESH,
        )
        counts2[link] += 1
        copy.start()
        sent.append(copy)

    weight_copy(0).wait_recv()
    for a, q in zip(MIXED, QS):
        scatter(2, FAR, 1, 2, a)
        scatter(0, DIAG3, 1, 1, q)
        scatter(1, DIAG1, 1, 3, q)
    weight_copy(1).wait_recv()
    weight_copy(2).wait_recv()
    for i, (a, b) in enumerate(zip(LOW, HIGH)):
        scatter(1, HALF, 0, 2, a, FAR)
        scatter(2, ACROSS, 1, 0, 2 * i, DIAG3, DIAG1)
        scatter(0, HALF, 0, 2, b, FAR)
        scatter(2, ACROSS, 1, 0, 2 * i + 1, DIAG3, DIAG1)
    for a, b in zip(LOW, HIGH):
        scatter(0, OWN3, 0, 1, a)
        scatter(1, OWN1, 0, 3, b)
    for a, b in zip(LOW, HIGH):
        scatter(0, OWN3, 0, 1, b, HALF)
        scatter(1, OWN1, 0, 3, a, HALF)
    for q in QS:
        total_ = sums(0, 0, q) + landed(ACROSS, q) + landed(OWN3, q) + landed(OWN1, q)
        out[here(q), :] = jnp.transpose(total_).astype(BF)

    for copy in sent:
        copy.wait_send()
    for s, j in ORDER:
        weighted_copy(s, j).wait_send()
    for i, who in enumerate((near, diag, sib)):
        exchange(i, who).wait_send()

    @pl.loop(1, 2 * NZ)
    def _(k):
        stat_copy(k).wait_send()

    for i in range(3):
        weight_copy(i).wait_send()


def body(images, ctf_table, group_ids, projections, log_prior):
    n_loc, pix = images.shape
    n_rows, width = projections.shape
    step = width // NQ
    dma = pltpu.SemaphoreType.DMA
    scratch = [
        pltpu.VMEM((4, n_loc, width), BF),
        pltpu.VMEM((2, 2, NX, n_loc, width), BF),
        pltpu.VMEM((2, NX, n_loc, width), BF),
        pltpu.VMEM((2, NX, NQ, n_rows, step), BF),
        pltpu.VMEM(ctf_table.shape, BF),
        pltpu.VMEM((2, NX, 16, width), BF),
        pltpu.VMEM((2, 16, PAD), BF),
        pltpu.VMEM((n_loc, n_rows), BF),
        pltpu.VMEM((2, 2, n_rows, PAD), F32),
        pltpu.VMEM((2, n_rows, 16), F32),
        pltpu.VMEM((3, n_rows, PAD), F32),
        pltpu.VMEM((3, n_rows, PAD), F32),
        pltpu.VMEM((2 * NZ, 8, PAD), F32),
        pltpu.VMEM((2, 2, n_rows, PAD), BF),
        pltpu.VMEM((2, NX, NQ, n_rows, step), BF),
        pltpu.VMEM((7, NQ, n_rows, step), BF),
        dma((4,)),
        dma((NQ + 1,)),
        dma((3, 3 * NQ)),
        dma((2, NX, NQ)),
        dma((2, NX)),
        dma((2, NX)),
        dma((2,)),
        dma((3,)),
        dma((3,)),
        dma((2 * NZ,)),
        dma((2 * NZ,)),
        dma((3,)),
        dma((3,)),
        dma((3, 3 * NQ)),
        dma((7, NQ)),
    ]
    vmem = pl.BlockSpec(memory_space=pltpu.VMEM)
    hbm = pl.BlockSpec(memory_space=pl.ANY)
    return pl.pallas_call(
        kernel,
        out_shape=jax.ShapeDtypeStruct((width, n_rows), BF),
        in_specs=[hbm, hbm, vmem, hbm, vmem],
        out_specs=vmem,
        scratch_shapes=scratch,
        compiler_params=pltpu.CompilerParams(
            collective_id=0, has_side_effects=True, vmem_limit_bytes=56 << 20
        ),
    )(images, ctf_table, group_ids.reshape(1, n_loc), projections, log_prior.reshape(1, n_rows))


def solution(mesh):
    placed = (P("dom", None), P(), P("dom"), P("orient", "dom"), P("orient"))
    return jax.shard_map(
        body, mesh=mesh, in_specs=placed, out_specs=P("dom", "orient"), check_vma=False
    )
```

time: 307 us -> 91.9 us (0.30)
  waiting for transfers between devices: 195 us -> 0 us
  Pallas kernels: 0 us -> 89.8 us
  blocking collectives: 50.8 us -> 0 us
  matrix products: 48.1 us -> 0 us
  between operations: 13.4 us -> 0.01 us
    reduce_scatter x1 -> x0, waiting for transfers between devices: 119 us -> none  [body(): lax.psum_scatter(rounded.astype(jnp.float32).astype(jnp.bfloat16), 'dom',...]
    pallas_call x0 -> x1, Pallas kernels: none -> 89.8 us  [body(): pl.pallas_call(kernel, out_shape=jax.ShapeDtypeStruct((width, n_rows), BF...]
    all_gather x1 -> x0, waiting for transfers between devices: 74.6 us -> none  [body(): piece = lax.all_gather(projections, 'dom', axis=1, tiled=True)]
    dot_general x5 -> x0, matrix products: 48.1 us -> none  [the longest x1 15.4 us: body(): lax.dot_general(ctf_square, piece_sq, (((1,), (1,)), ((), ())), precision...]
    pmax x1 -> x0, blocking collectives: 26.9 us -> none  [body(): top = lax.pmax(jnp.max(scores, axis=1), 'orient')]
    psum x1 -> x0, blocking collectives: 23.9 us -> none  [body(): total = lax.psum(jnp.sum(expo, axis=1), 'orient')]
  transfers between devices with their start and end apart: 2 -> 0, of which waited for: 2 -> 0; matrix products, arithmetic and copies ran while one was open for 3% -> 0% of each run, Pallas kernels for 0% -> 0%
where the time goes in v1:
time: 91.9 us; the launch traced here: 91.7 us
  Pallas kernels  89.8 us (98%)
  local copies, waits for them, and re-layouts  1.87 us (2%)
    pallas_call x1, Pallas kernels, body(): pl.pallas_call(kernel, out_shape=jax.ShapeDtypeStruct((width, n_rows), BF...  89.8 us
    unnamed x1, local copies, waits for them, and re-layouts  1.87 us

profile of v1, /device:TPU:1, one launch (start us, length us, event | category | flops | bytes accessed | tf_op | source)
XLA Modules:
  0.0 91.7 jit_solution(7336925494624340765)
XLA Ops:
  0.0 89.8 %shard_map.55 = bf16[2048,128]{1,0:T(8,128)(2,1)} custom-call(bf16[176,32768]{1,0:T(8,128)(2,1)} %images.1, bf16[8,32768]{1,0:T(8,128)(2,1)} %ctf.1, s32[1,176]{1,0:T(1,128)} %bitcast.2, bf16[128,2048]{1,0:T(8,128)(2,1)} %proj.1, f32[1,128]{1,0:T(1,128)} %bitcast.3), custom_call_target="tpu_custom_call" | custom-call | tf_op jit(solution)/shard_map/pallas_call | solution.py:477
  89.8 1.9 %copy.7 = bf16[2048,128]{1,0:T(8,128)(2,1)} copy(bf16[2048,128]{1,0:T(8,128)(2,1)} %shard_map.55) | data formatting | bytes 1048576

commit v2 on v1

--- a/solution.py
+++ b/solution.py
@@ -12,13 +12,14 @@
 F32 = jnp.float32
 MESH = pl.DeviceIdType.MESH
 NX, NZ = 4, 8
+SHARES = (4, 4, 4, 2, 2)
+LOW, HIGH, VIA = (0, 1), (2, 3, 4), 4
+PIECES = (0, 1, 2, 3, 4)
+MIXED = (0, 2, 1, 3, 4)
 NQ = 4
-LOW, HIGH = (0, 1), (2, 3)
-QS = (0, 1, 2, 3)
-MIXED = (0, 2, 1, 3)
 PAD = 256
 ORDER = ((0, 0), (0, 3), (0, 1), (1, 0), (0, 2), (1, 2), (1, 3), (1, 1))
-FAR, DIAG3, DIAG1, OWN3, OWN1, ACROSS, HALF = range(7)
+FAR, DIAG3, DIAG1, OWN3, OWN1, ACROSS, HALF, VIA1, VIA3 = range(9)
 
 
 def nt(a, b):
@@ -78,6 +79,10 @@
     n_loc, pix = images.shape
     n_rows, width = proj.shape
     step = width // NQ
+
+    def piece(p):
+        return pl.ds(sum(SHARES[:p]) * width // 16, SHARES[p] * width // 16)
+
     scale = float(np.float32(1.0) / np.sqrt(np.float32(pix)))
     dom, ori = lax.axis_index("dom"), lax.axis_index("orient")
     yh, x, core = dom // (2 * NX), lax.rem(dom // 2, NX), lax.rem(dom, 2)
@@ -111,18 +116,12 @@
             images.at[:, pl.ds(start, width)], raw.at[i % n_raw], raw_sem.at[i % n_raw]
         )
 
-    ctf_copy = pltpu.make_async_copy(ctf, ctfv, loc_sem.at[NQ])
+    ctf_copy = pltpu.make_async_copy(ctf, ctfv, loc_sem.at[1])
     ctf_copy.start()
     for i in range(n_raw):
         raw_copy(i).start()
-    own_copies = [
-        pltpu.make_async_copy(
-            proj.at[:, pl.ds(q * step, step)], blocks.at[0, 0, q], loc_sem.at[q]
-        )
-        for q in QS
-    ]
-    for copy in own_copies:
-        copy.start()
+    own_copy = pltpu.make_async_copy(proj, blocks.at[0, 0], loc_sem.at[0])
+    own_copy.start()
 
     barrier = pltpu.get_barrier_semaphore()
     for who in (xp, xm, yp, sib, diag):
@@ -138,12 +137,12 @@
     counts = [0, 0, 0]
     sent = []
 
-    def gather(link, src, s, j, q):
+    def gather(link, src, s, j, p):
         copy = pltpu.make_async_remote_copy(
-            src_ref=src,
-            dst_ref=blocks.at[s, j, q],
+            src_ref=src.at[:, piece(p)],
+            dst_ref=blocks.at[s, j, :, piece(p)],
             send_sem=g_send.at[link, counts[link]],
-            recv_sem=g_recv.at[s, j, q],
+            recv_sem=g_recv.at[s, j, p],
             device_id=links[link],
             device_id_type=MESH,
         )
@@ -151,20 +150,21 @@
         copy.start()
         sent.append(copy)
 
-    def arrived(s, j, q):
+    def arrived(s, j, p):
+        here = blocks.at[s, j, :, piece(p)]
         pltpu.make_async_remote_copy(
-            src_ref=blocks.at[s, j, q],
-            dst_ref=blocks.at[s, j, q],
+            src_ref=here,
+            dst_ref=here,
             send_sem=g_send.at[0, 0],
-            recv_sem=g_recv.at[s, j, q],
+            recv_sem=g_recv.at[s, j, p],
             device_id=xp,
             device_id_type=MESH,
         ).wait_recv()
 
     for a, b in zip(LOW + HIGH, HIGH + LOW):
-        gather(0, proj.at[:, pl.ds(a * step, step)], 0, 3, a)
-        gather(1, proj.at[:, pl.ds(b * step, step)], 0, 1, b)
-        gather(2, proj.at[:, pl.ds(a * step, step)], 1, 0, a)
+        gather(0, proj, 0, 3, a)
+        gather(1, proj, 0, 1, b)
+        gather(2, proj, 1, 0, a)
 
     group = lax.broadcasted_iota(jnp.int32, (n_rows, n_loc), 0)
     hot_full = jnp.where(group == gids[...], 1.0, 0.0)
@@ -191,7 +191,7 @@
         d = pixel_block(s, j, core if own else 1 - core)
         dst = weighted.at[0, s, j] if own else stage.at[s, j]
         raw_copy(i).wait()
-        tile = 256
+        tile = 1024
 
         @pl.loop(0, width // tile)
         def _(t):
@@ -223,9 +223,8 @@
             device_id_type=MESH,
         )
 
-    def score(s, j, q):
-        here = pl.ds(pl.multiple_of(q * step, step), step)
-        block = blocks[s, j, q]
+    def score(s, j, here):
+        block = blocks[s, j, :, here]
         for nb in (0, 1):
             acc[s, nb, :, :n_loc] += nt(block, weighted[nb, s, j, :, here])
         wide = block.astype(F32)
@@ -238,35 +237,42 @@
     def score_block(s, j):
         @pl.loop(0, NQ)
         def _(q):
-            score(s, j, q)
+            score(s, j, pl.ds(pl.multiple_of(q * step, step), step))
 
     for i in range(8):
         weigh(i)
-    for a, b in zip(LOW, HIGH):
-        arrived(0, 3, a)
-        gather(0, blocks.at[0, 3, a], 0, 2, a)
-        arrived(0, 1, b)
-        gather(1, blocks.at[0, 1, b], 0, 2, b)
+    for p in LOW:
+        arrived(0, 3, p)
+        gather(0, blocks.at[0, 3], 0, 2, p)
+    for p in HIGH:
+        arrived(0, 1, p)
+        gather(1, blocks.at[0, 1], 0, 2, p)
     for i in range(8, 16):
         weigh(i)
-    for q in QS:
-        arrived(1, 0, q)
-        gather(0, blocks.at[1, 0, q], 1, 3, q)
-        gather(1, blocks.at[1, 0, q], 1, 1, q)
-    for copy in own_copies:
-        copy.wait()
+    gather(2, blocks.at[0, 1], 1, 1, VIA)
+    for p in PIECES:
+        arrived(1, 0, p)
+        if p != VIA:
+            gather(0, blocks.at[1, 0], 1, 3, p)
+            gather(1, blocks.at[1, 0], 1, 1, p)
+    for p in HIGH:
+        arrived(0, 3, p)
+    gather(2, blocks.at[0, 3], 1, 3, VIA)
+    for p in LOW:
+        arrived(0, 1, p)
+    own_copy.wait()
     weighted_copy(0, 0).wait_recv()
     score_block(0, 0)
-    for a, b in zip(LOW, HIGH):
-        arrived(0, 3, b)
-        arrived(0, 1, a)
+    for p in MIXED[:2]:
+        arrived(0, 2, p)
+        gather(2, blocks.at[0, 2], 1, 2, p)
     weighted_copy(0, 3).wait_recv()
     score_block(0, 3)
+    for p in MIXED[2:]:
+        arrived(0, 2, p)
+        gather(2, blocks.at[0, 2], 1, 2, p)
     weighted_copy(0, 1).wait_recv()
     score_block(0, 1)
-    for q in MIXED:
-        arrived(0, 2, q)
-        gather(2, blocks.at[0, 2, q], 1, 2, q)
     weighted_copy(0, 2).wait_recv()
     score_block(0, 2)
 
@@ -297,13 +303,18 @@
     score_block(1, 0)
     for j in (2, 3, 1):
         weighted_copy(1, j).wait_recv()
-    for a, q in zip(MIXED, QS):
+    arrived(1, 1, VIA)
+    score(1, 1, piece(VIA))
+    arrived(1, 3, VIA)
+    score(1, 3, piece(VIA))
+    for a, p in zip(MIXED, PIECES):
+        if p != VIA:
+            arrived(1, 3, p)
+            score(1, 3, piece(p))
+            arrived(1, 1, p)
+            score(1, 1, piece(p))
         arrived(1, 2, a)
-        score(1, 2, a)
-        arrived(1, 3, q)
-        score(1, 3, q)
-        arrived(1, 1, q)
-        score(1, 1, q)
+        score(1, 2, piece(a))
 
     xsend[2] = partial_scores(1, 1)
     exchange(2, sib).start()
@@ -316,9 +327,8 @@
 
     largest = jnp.max(scores, axis=0, keepdims=True)
     expo = jnp.exp(scores - largest)
-    stat[0, 0:1] = largest
-    stat[0, 1:2] = jnp.sum(expo, axis=0, keepdims=True)
-    stat[0, 2:8] = jnp.zeros((6, PAD), F32)
+    stat[0, :, :PAD] = largest
+    stat[0, :, PAD:] = jnp.sum(expo, axis=0, keepdims=True)
 
     def stat_copy(k):
         return pltpu.make_async_remote_copy(
@@ -338,9 +348,12 @@
     def _(k):
         stat_copy(k).wait_recv()
 
-    tops = stat[:, 0, :]
-    top = jnp.max(tops, axis=0, keepdims=True)
-    total = jnp.sum(stat[:, 1, :] * jnp.exp(tops - top), axis=0, keepdims=True)
+    top, total = largest, stat[0, :, PAD:]
+    for k in range(1, 2 * NZ):
+        top = jnp.maximum(top, stat[k, :, :PAD])
+    total = jnp.zeros_like(top)
+    for k in range(2 * NZ):
+        total += stat[k, :, PAD:] * jnp.exp(stat[k, :, :PAD] - top)
     wts[1, 0] = (expo * (jnp.exp(largest - top) / total)).astype(BF)
 
     def weight_copy(i):
@@ -359,37 +372,33 @@
 
     counts2 = [0, 0, 0]
 
-    def here(q):
-        return pl.ds(q * step, step)
-
-    def sums(s, j, q):
-        return nn(wts[s, 0, :, :n_loc], weighted[0, s, j, :, here(q)]) + nn(
-            wts[s, 1, :, :n_loc], weighted[1, s, j, :, here(q)]
-        )
-
-    def landed(kind, q):
+    def sums(s, j, p):
+        return nn(wts[s, 0, :, :n_loc], weighted[0, s, j, :, piece(p)]) + nn(
+            wts[s, 1, :, :n_loc], weighted[1, s, j, :, piece(p)]
+        )
+
+    def landed(kind, p):
+        here = rx.at[kind, :, piece(p)]
         pltpu.make_async_remote_copy(
-            src_ref=rx.at[kind, q],
-            dst_ref=rx.at[kind, q],
+            src_ref=here,
+            dst_ref=here,
             send_sem=r_send.at[0, 0],
-            recv_sem=r_recv.at[kind, q],
+            recv_sem=r_recv.at[kind, p],
             device_id=xp,
             device_id_type=MESH,
         ).wait_recv()
-        return rx[kind, q].astype(F32)
-
-    def scatter(link, kind, s, j, q, *added):
+        return rx[kind, :, piece(p)].astype(F32)
+
+    def scatter(link, kind, s, j, p, *added):
+        total_ = sums(s, j, p)
         for k in added:
-            pass
-        total_ = sums(s, j, q)
-        for k in added:
-            total_ = total_ + landed(k, q)
-        part[s, j, q] = total_.astype(BF)
+            total_ = total_ + landed(k, p)
+        part[s, j, :, piece(p)] = total_.astype(BF)
         copy = pltpu.make_async_remote_copy(
-            src_ref=part.at[s, j, q],
-            dst_ref=rx.at[kind, q],
+            src_ref=part.at[s, j, :, piece(p)],
+            dst_ref=rx.at[kind, :, piece(p)],
             send_sem=r_send.at[link, counts2[link]],
-            recv_sem=r_recv.at[kind, q],
+            recv_sem=r_recv.at[kind, p],
             device_id=links[link],
             device_id_type=MESH,
         )
@@ -398,26 +407,38 @@
         sent.append(copy)
 
     weight_copy(0).wait_recv()
-    for a, q in zip(MIXED, QS):
+    for a, p in zip(MIXED, PIECES):
         scatter(2, FAR, 1, 2, a)
-        scatter(0, DIAG3, 1, 1, q)
-        scatter(1, DIAG1, 1, 3, q)
+        if p != VIA:
+            scatter(0, DIAG3, 1, 1, p)
+            scatter(1, DIAG1, 1, 3, p)
+    scatter(2, VIA3, 1, 3, VIA)
+    scatter(2, VIA1, 1, 1, VIA)
     weight_copy(1).wait_recv()
     weight_copy(2).wait_recv()
-    for i, (a, b) in enumerate(zip(LOW, HIGH)):
-        scatter(1, HALF, 0, 2, a, FAR)
-        scatter(2, ACROSS, 1, 0, 2 * i, DIAG3, DIAG1)
-        scatter(0, HALF, 0, 2, b, FAR)
-        scatter(2, ACROSS, 1, 0, 2 * i + 1, DIAG3, DIAG1)
-    for a, b in zip(LOW, HIGH):
-        scatter(0, OWN3, 0, 1, a)
-        scatter(1, OWN1, 0, 3, b)
-    for a, b in zip(LOW, HIGH):
-        scatter(0, OWN3, 0, 1, b, HALF)
-        scatter(1, OWN1, 0, 3, a, HALF)
-    for q in QS:
-        total_ = sums(0, 0, q) + landed(ACROSS, q) + landed(OWN3, q) + landed(OWN1, q)
-        out[here(q), :] = jnp.transpose(total_).astype(BF)
+    scatter(1, HALF, 0, 2, 0, FAR)
+    scatter(2, ACROSS, 1, 0, 0, DIAG3, DIAG1)
+    scatter(0, HALF, 0, 2, 2, FAR)
+    scatter(2, ACROSS, 1, 0, 1, DIAG3, DIAG1)
+    scatter(1, HALF, 0, 2, 1, FAR)
+    scatter(2, ACROSS, 1, 0, 2, DIAG3, DIAG1)
+    scatter(0, HALF, 0, 2, 3, FAR)
+    scatter(2, ACROSS, 1, 0, 3, DIAG3, DIAG1)
+    scatter(2, ACROSS, 1, 0, 4)
+    scatter(0, HALF, 0, 2, 4, FAR)
+    scatter(0, OWN3, 0, 1, 0)
+    scatter(1, OWN1, 0, 3, 2)
+    scatter(0, OWN3, 0, 1, 1)
+    scatter(1, OWN1, 0, 3, 3)
+    scatter(1, OWN1, 0, 3, 4, VIA3)
+    scatter(1, OWN1, 0, 3, 0, HALF)
+    scatter(0, OWN3, 0, 1, 2, HALF)
+    scatter(1, OWN1, 0, 3, 1, HALF)
+    scatter(0, OWN3, 0, 1, 3, HALF)
+    scatter(0, OWN3, 0, 1, 4, HALF, VIA1)
+    for p in (2, 3, 4, 0, 1):
+        total_ = sums(0, 0, p) + landed(ACROSS, p) + landed(OWN3, p) + landed(OWN1, p)
+        out[piece(p), :] = jnp.transpose(total_).astype(BF)
 
     for copy in sent:
         copy.wait_send()
@@ -437,13 +458,12 @@
 def body(images, ctf_table, group_ids, projections, log_prior):
     n_loc, pix = images.shape
     n_rows, width = projections.shape
-    step = width // NQ
     dma = pltpu.SemaphoreType.DMA
     scratch = [
         pltpu.VMEM((4, n_loc, width), BF),
         pltpu.VMEM((2, 2, NX, n_loc, width), BF),
         pltpu.VMEM((2, NX, n_loc, width), BF),
-        pltpu.VMEM((2, NX, NQ, n_rows, step), BF),
+        pltpu.VMEM((2, NX, n_rows, width), BF),
         pltpu.VMEM(ctf_table.shape, BF),
         pltpu.VMEM((2, NX, 16, width), BF),
         pltpu.VMEM((2, 16, PAD), BF),
@@ -452,14 +472,14 @@
         pltpu.VMEM((2, n_rows, 16), F32),
         pltpu.VMEM((3, n_rows, PAD), F32),
         pltpu.VMEM((3, n_rows, PAD), F32),
-        pltpu.VMEM((2 * NZ, 8, PAD), F32),
+        pltpu.VMEM((2 * NZ, 1, 2 * PAD), F32),
         pltpu.VMEM((2, 2, n_rows, PAD), BF),
-        pltpu.VMEM((2, NX, NQ, n_rows, step), BF),
-        pltpu.VMEM((7, NQ, n_rows, step), BF),
+        pltpu.VMEM((2, NX, n_rows, width), BF),
+        pltpu.VMEM((9, n_rows, width), BF),
         dma((4,)),
-        dma((NQ + 1,)),
-        dma((3, 3 * NQ)),
-        dma((2, NX, NQ)),
+        dma((2,)),
+        dma((3, 12)),
+        dma((2, NX, len(SHARES))),
         dma((2, NX)),
         dma((2, NX)),
         dma((2,)),
@@ -469,8 +489,8 @@
         dma((2 * NZ,)),
         dma((3,)),
         dma((3,)),
-        dma((3, 3 * NQ)),
-        dma((7, NQ)),
+        dma((3, 13)),
+        dma((9, len(SHARES))),
     ]
     vmem = pl.BlockSpec(memory_space=pltpu.VMEM)
     hbm = pl.BlockSpec(memory_space=pl.ANY)

time: 91.9 us -> 81.9 us (0.89)
  Pallas kernels: 89.8 us -> 79.9 us
    pallas_call x1, Pallas kernels: 89.8 us -> 79.9 us  [body(): pl.pallas_call(kernel, out_shape=jax.ShapeDtypeStruct((width, n_rows), BF...]
where the time goes in v2:
time: 81.9 us; the launch traced here: 81.8 us
  Pallas kernels  79.9 us (98%)
  local copies, waits for them, and re-layouts  1.87 us (2%)
    pallas_call x1, Pallas kernels, body(): pl.pallas_call(kernel, out_shape=jax.ShapeDtypeStruct((width, n_rows), BF...  79.9 us
    unnamed x1, local copies, waits for them, and re-layouts  1.87 us

profile of v2, /device:TPU:1, one launch (start us, length us, event | category | flops | bytes accessed | tf_op | source)
XLA Modules:
  0.0 81.8 jit_solution(17508737802437828546)
XLA Ops:
  0.0 79.9 %shard_map.55 = bf16[2048,128]{1,0:T(8,128)(2,1)} custom-call(bf16[176,32768]{1,0:T(8,128)(2,1)} %images.1, bf16[8,32768]{1,0:T(8,128)(2,1)} %ctf.1, s32[1,176]{1,0:T(1,128)} %bitcast.2, bf16[128,2048]{1,0:T(8,128)(2,1)} %proj.1, f32[1,128]{1,0:T(1,128)} %bitcast.3), custom_call_target="tpu_custom_call" | custom-call | tf_op jit(solution)/shard_map/pallas_call | solution.py:497
  79.9 1.9 %copy.7 = bf16[2048,128]{1,0:T(8,128)(2,1)} copy(bf16[2048,128]{1,0:T(8,128)(2,1)} %shard_map.55) | data formatting | bytes 1048576

commit v3 on v2

--- a/solution.py
+++ b/solution.py
@@ -12,10 +12,12 @@
 F32 = jnp.float32
 MESH = pl.DeviceIdType.MESH
 NX, NZ = 4, 8
-SHARES = (4, 4, 4, 2, 2)
-LOW, HIGH, VIA = (0, 1), (2, 3, 4), 4
-PIECES = (0, 1, 2, 3, 4)
-MIXED = (0, 2, 1, 3, 4)
+SHARES = (2, 2, 4, 2, 2, 4)
+LOW, HIGH = (0, 1, 2), (3, 4, 5)
+PIECES = (0, 1, 2, 3, 4, 5)
+MIXED = (0, 3, 1, 4, 2, 5)
+LATE = (2, 5, 0, 1, 3, 4)
+FOLD = (2, 5)
 NQ = 4
 PAD = 256
 ORDER = ((0, 0), (0, 3), (0, 1), (1, 0), (0, 2), (1, 2), (1, 3), (1, 1))
@@ -60,6 +62,14 @@
     wts,
     part,
     rx,
+    far_raw,
+    far_out,
+    far,
+    wts_far,
+    begun,
+    final,
+    turned,
+    out_sem,
     raw_sem,
     loc_sem,
     g_send,
@@ -75,6 +85,12 @@
     wt_recv,
     r_send,
     r_recv,
+    f_raw,
+    f_send,
+    f_recv,
+    fy_send,
+    wf_send,
+    wf_recv,
 ):
     n_loc, pix = images.shape
     n_rows, width = proj.shape
@@ -97,6 +113,8 @@
     sib = device(yh, x, 1 - core, yl)
     near = device(yh, x, core, 1 - yl)
     diag = device(yh, x, 1 - core, 1 - yl)
+    yd = device(1 - yh, x, 1 - core, 1 - yl)
+    fold = SHARES[FOLD[0]] * width // 16
 
     def peer(k):
         return {"dom": dom, "orient": lax.rem(ori + k, 2 * NZ)}
@@ -104,6 +122,14 @@
     def pixel_block(s, j, core_):
         yh_ = yh if s == 0 else 1 - yh
         return (yh_ * NX + lax.rem(x + j, NX)) * 2 + core_
+
+    barrier = pltpu.get_barrier_semaphore()
+    for who in (xp, xm, yp, sib, diag, yd):
+        pl.semaphore_signal(barrier, inc=1, device_id=who, device_id_type=MESH)
+
+    @pl.loop(1, 2 * NZ)
+    def _(k):
+        pl.semaphore_signal(barrier, inc=1, device_id=peer(k), device_id_type=MESH)
 
     jobs = [(s, j, own) for s, j in ORDER for own in (0, 1)]
     n_raw = raw.shape[0]
@@ -118,20 +144,23 @@
 
     ctf_copy = pltpu.make_async_copy(ctf, ctfv, loc_sem.at[1])
     ctf_copy.start()
+
+    def far_start(r):
+        d = pixel_block(1, z // 2, core if r == 0 else 1 - core)
+        return pl.multiple_of(d * width + width // 4 + lax.rem(z, 2) * (width // 2), fold)
+
+    far_loads = [
+        pltpu.make_async_copy(images.at[:, pl.ds(far_start(r), fold)], far_raw.at[r], f_raw.at[r])
+        for r in (0, 1)
+    ]
+    for copy in far_loads:
+        copy.start()
     for i in range(n_raw):
         raw_copy(i).start()
     own_copy = pltpu.make_async_copy(proj, blocks.at[0, 0], loc_sem.at[0])
     own_copy.start()
 
-    barrier = pltpu.get_barrier_semaphore()
-    for who in (xp, xm, yp, sib, diag):
-        pl.semaphore_signal(barrier, inc=1, device_id=who, device_id_type=MESH)
-
-    @pl.loop(1, 2 * NZ)
-    def _(k):
-        pl.semaphore_signal(barrier, inc=1, device_id=peer(k), device_id_type=MESH)
-
-    pl.semaphore_wait(barrier, 5 + 2 * NZ - 1)
+    pl.semaphore_wait(barrier, 6 + 2 * NZ - 1)
 
     links = (xp, xm, yp)
     counts = [0, 0, 0]
@@ -164,7 +193,9 @@
     for a, b in zip(LOW + HIGH, HIGH + LOW):
         gather(0, proj, 0, 3, a)
         gather(1, proj, 0, 1, b)
-        gather(2, proj, 1, 0, a)
+
+    for p in (0, 1):
+        gather(2, proj, 1, 0, p)
 
     group = lax.broadcasted_iota(jnp.int32, (n_rows, n_loc), 0)
     hot_full = jnp.where(group == gids[...], 1.0, 0.0)
@@ -186,6 +217,78 @@
     norm[...] = jnp.zeros(norm.shape, F32)
     ctf_copy.wait()
 
+    half = fold // 2
+
+    def unit(u):
+        return pl.ds(u * half, half)
+
+    def far_first(r, u):
+        return pltpu.make_async_remote_copy(
+            src_ref=far_out.at[r, :, unit(u)],
+            dst_ref=far.at[z, 1 - yl, :, unit(u)],
+            send_sem=fy_send.at[r, u],
+            recv_sem=f_recv.at[0, 0, u],
+            device_id=(yp, yd)[r],
+            device_id_type=MESH,
+        )
+
+    for r in (0, 1):
+        far_loads[r].wait()
+        rows = nn(hot_t[:, :8], ctfv[:, pl.ds(far_start(r), fold)])
+        far_out[r] = (rows * far_raw[r].astype(F32)).astype(BF)
+
+    @pl.when(core == 1 - yl)
+    def _():
+        for u in (0, 1):
+            for r in (0, 1):
+                far_first(r, u).start()
+
+    for p in (2, 5, 3, 4):
+        gather(2, proj, 1, 0, p)
+
+    around = (peer(2), peer(2 * NZ - 2), near)
+    counts_f = [0, 0, 0]
+
+    def far_ref(dz, side, u):
+        return far.at[lax.rem(z + dz, NZ), yl if side == 0 else 1 - yl, :, unit(u)]
+
+    def far_on(link, dz, side, u):
+        target_dz = (dz + (NZ - 1, 1, 0)[link]) % NZ
+        target_side = 1 - side if link == 2 else side
+        copy = pltpu.make_async_remote_copy(
+            src_ref=far_ref(dz, side, u),
+            dst_ref=far_ref(dz, side, u),
+            send_sem=f_send.at[link, counts_f[link]],
+            recv_sem=f_recv.at[target_side, target_dz, u],
+            device_id=around[link],
+            device_id_type=MESH,
+        )
+        counts_f[link] += 1
+        copy.start()
+        sent.append(copy)
+
+    waited = set()
+
+    def far_in(dz, side, u):
+        waited.add((dz, side, u))
+        pltpu.make_async_remote_copy(
+            src_ref=far_ref(dz, side, u),
+            dst_ref=far_ref(dz, side, u),
+            send_sem=f_send.at[0, 0],
+            recv_sem=f_recv.at[side, dz, u],
+            device_id=near,
+            device_id_type=MESH,
+        ).wait_recv()
+
+    def far_step(dz, side, units=(0, 1), to_near=True):
+        for u in units:
+            for link, d in ((0, (NZ - dz) % NZ), (1, dz)):
+                if dz or link == 0:
+                    far_in(d, side, u)
+                far_on(link, d, side, u)
+                if to_near and (dz or link == 0):
+                    far_on(2, d, side, u)
+
     def weigh(i):
         s, j, own = jobs[i]
         d = pixel_block(s, j, core if own else 1 - core)
@@ -239,7 +342,7 @@
         def _(q):
             score(s, j, pl.ds(pl.multiple_of(q * step, step), step))
 
-    for i in range(8):
+    for i in range(6):
         weigh(i)
     for p in LOW:
         arrived(0, 3, p)
@@ -247,34 +350,40 @@
     for p in HIGH:
         arrived(0, 1, p)
         gather(1, blocks.at[0, 1], 0, 2, p)
-    for i in range(8, 16):
+    far_step(0, 0)
+    for i in range(6, 11):
         weigh(i)
-    gather(2, blocks.at[0, 1], 1, 1, VIA)
-    for p in PIECES:
+    far_step(1, 0)
+    for i in range(11, 16):
+        weigh(i)
+    for p in MIXED[:2]:
+        arrived(0, 2, p)
+        gather(2, blocks.at[0, 2], 1, 2, p)
+    for p in LATE:
         arrived(1, 0, p)
-        if p != VIA:
-            gather(0, blocks.at[1, 0], 1, 3, p)
-            gather(1, blocks.at[1, 0], 1, 1, p)
+        gather(0, blocks.at[1, 0], 1, 3, p)
+        gather(1, blocks.at[1, 0], 1, 1, p)
+    for p in MIXED[2:4]:
+        arrived(0, 2, p)
+        gather(2, blocks.at[0, 2], 1, 2, p)
+    far_step(2, 0)
+    for p in MIXED[4:]:
+        arrived(0, 2, p)
+        gather(2, blocks.at[0, 2], 1, 2, p)
     for p in HIGH:
         arrived(0, 3, p)
-    gather(2, blocks.at[0, 3], 1, 3, VIA)
     for p in LOW:
         arrived(0, 1, p)
     own_copy.wait()
     weighted_copy(0, 0).wait_recv()
     score_block(0, 0)
-    for p in MIXED[:2]:
-        arrived(0, 2, p)
-        gather(2, blocks.at[0, 2], 1, 2, p)
-    weighted_copy(0, 3).wait_recv()
-    score_block(0, 3)
-    for p in MIXED[2:]:
-        arrived(0, 2, p)
-        gather(2, blocks.at[0, 2], 1, 2, p)
-    weighted_copy(0, 1).wait_recv()
-    score_block(0, 1)
-    weighted_copy(0, 2).wait_recv()
-    score_block(0, 2)
+    far_in(NZ - 3, 0, 0)
+    far_on(0, NZ - 3, 0, 0)
+    far_in(3, 0, 1)
+    far_on(1, 3, 0, 1)
+    for j in (3, 1, 2):
+        weighted_copy(0, j).wait_recv()
+        score_block(0, j)
 
     hot_copy.wait()
 
@@ -299,22 +408,34 @@
     exchange(0, near).start()
     exchange(1, diag).start()
 
+    far_step(2, 1, units=(0,), to_near=False)
     weighted_copy(1, 0).wait_recv()
     score_block(1, 0)
     for j in (2, 3, 1):
         weighted_copy(1, j).wait_recv()
-    arrived(1, 1, VIA)
-    score(1, 1, piece(VIA))
-    arrived(1, 3, VIA)
-    score(1, 3, piece(VIA))
-    for a, p in zip(MIXED, PIECES):
-        if p != VIA:
-            arrived(1, 3, p)
-            score(1, 3, piece(p))
-            arrived(1, 1, p)
-            score(1, 1, piece(p))
-        arrived(1, 2, a)
-        score(1, 2, piece(a))
+
+    def score_far(p):
+        arrived(1, 2, p)
+        score(1, 2, piece(p))
+
+    def score_late(p):
+        for j in (3, 1):
+            arrived(1, j, p)
+            score(1, j, piece(p))
+
+    score_far(0)
+    score_far(3)
+    score_late(2)
+    score_far(1)
+    score_far(4)
+    far_step(2, 1, units=(1,), to_near=False)
+    score_late(5)
+    score_far(2)
+    score_late(0)
+    score_late(1)
+    score_far(5)
+    score_late(3)
+    score_late(4)
 
     xsend[2] = partial_scores(1, 1)
     exchange(2, sib).start()
@@ -340,9 +461,12 @@
             device_id_type=MESH,
         )
 
-    @pl.loop(1, 2 * NZ)
-    def _(k):
+    for k in sorted(range(1, 2 * NZ), key=lambda k: abs(k - NZ)):
         stat_copy(k).start()
+    far_in(NZ - 3, 1, 0)
+    far_on(0, NZ - 3, 1, 0)
+    far_in(3, 1, 1)
+    far_on(1, 3, 1, 1)
 
     @pl.loop(1, 2 * NZ)
     def _(k):
@@ -367,15 +491,43 @@
             device_id_type=MESH,
         )
 
-    for i in range(3):
-        weight_copy(i).start()
+    def fold_copy(i):
+        return pltpu.make_async_remote_copy(
+            src_ref=wts.at[1, 0],
+            dst_ref=wts_far.at[core],
+            send_sem=wf_send.at[i],
+            recv_sem=wf_recv.at[i],
+            device_id=(yp, yd)[i],
+            device_id_type=MESH,
+        )
+
+    def fold_landed(i):
+        here = wts_far.at[core if i == 0 else 1 - core]
+        pltpu.make_async_remote_copy(
+            src_ref=here,
+            dst_ref=here,
+            send_sem=wf_send.at[i],
+            recv_sem=wf_recv.at[i],
+            device_id=yp,
+            device_id_type=MESH,
+        ).wait_recv()
+
+    weight_copy(0).start()
+    fold_copy(0).start()
+    fold_copy(1).start()
+    weight_copy(1).start()
+    weight_copy(2).start()
 
     counts2 = [0, 0, 0]
 
     def sums(s, j, p):
-        return nn(wts[s, 0, :, :n_loc], weighted[0, s, j, :, piece(p)]) + nn(
+        total_ = nn(wts[s, 0, :, :n_loc], weighted[0, s, j, :, piece(p)]) + nn(
             wts[s, 1, :, :n_loc], weighted[1, s, j, :, piece(p)]
         )
+        if s == 0 and p in FOLD:
+            for nb in (0, 1):
+                total_ += nn(wts_far[nb, :, :n_loc], far[2 * j + FOLD.index(p), nb])
+        return total_
 
     def landed(kind, p):
         here = rx.at[kind, :, piece(p)]
@@ -389,8 +541,11 @@
         ).wait_recv()
         return rx[kind, :, piece(p)].astype(F32)
 
-    def scatter(link, kind, s, j, p, *added):
-        total_ = sums(s, j, p)
+    def scatter(link, kind, s, j, p, *added, begun=None):
+        if begun is None:
+            total_ = sums(s, j, p)
+        else:
+            total_ = begun + nn(wts[s, 1, :, :n_loc], weighted[1, s, j, :, piece(p)])
         for k in added:
             total_ = total_ + landed(k, p)
         part[s, j, :, piece(p)] = total_.astype(BF)
@@ -406,39 +561,65 @@
         copy.start()
         sent.append(copy)
 
+    first = [(0, DIAG3, 1, 1, 0), (1, DIAG1, 1, 3, 3)]
+    for i, (_, _, s, j, p) in enumerate(first):
+        begun[i] = nn(wts[s, 0, :, :n_loc], weighted[0, s, j, :, piece(p)])
     weight_copy(0).wait_recv()
-    for a, p in zip(MIXED, PIECES):
-        scatter(2, FAR, 1, 2, a)
-        if p != VIA:
-            scatter(0, DIAG3, 1, 1, p)
-            scatter(1, DIAG1, 1, 3, p)
-    scatter(2, VIA3, 1, 3, VIA)
-    scatter(2, VIA1, 1, 1, VIA)
+    for i, job in enumerate(first):
+        scatter(*job, begun=begun[i])
+    scatter(0, DIAG3, 1, 1, 3)
+    scatter(1, DIAG1, 1, 3, 0)
+    scatter(2, FAR, 1, 2, 3)
+    scatter(2, FAR, 1, 2, 0)
     weight_copy(1).wait_recv()
     weight_copy(2).wait_recv()
+    scatter(0, OWN3, 0, 1, 0)
+    scatter(1, OWN1, 0, 3, 3)
+    scatter(2, FAR, 1, 2, 4)
+    scatter(2, FAR, 1, 2, 1)
+    for side in (0, 1):
+        for dz in range(NZ):
+            for u in (0, 1):
+                if (dz, side, u) not in waited:
+                    far_in(dz, side, u)
+    fold_landed(0)
+    fold_landed(1)
+    scatter(0, OWN3, 0, 1, 2)
+    scatter(1, OWN1, 0, 3, 5)
+    scatter(2, VIA1, 1, 1, 1)
+    scatter(2, VIA3, 1, 3, 4)
+    scatter(0, HALF, 0, 2, 3, FAR)
     scatter(1, HALF, 0, 2, 0, FAR)
+    scatter(2, VIA1, 1, 1, 4)
+    scatter(2, VIA3, 1, 3, 1)
+    scatter(0, HALF, 0, 2, 5)
+    scatter(1, HALF, 0, 2, 2)
+    scatter(0, HALF, 0, 2, 4, FAR)
+    scatter(1, HALF, 0, 2, 1, FAR)
     scatter(2, ACROSS, 1, 0, 0, DIAG3, DIAG1)
-    scatter(0, HALF, 0, 2, 2, FAR)
-    scatter(2, ACROSS, 1, 0, 1, DIAG3, DIAG1)
-    scatter(1, HALF, 0, 2, 1, FAR)
-    scatter(2, ACROSS, 1, 0, 2, DIAG3, DIAG1)
-    scatter(0, HALF, 0, 2, 3, FAR)
     scatter(2, ACROSS, 1, 0, 3, DIAG3, DIAG1)
+    scatter(0, OWN3, 0, 1, 1, VIA1)
+    scatter(1, OWN1, 0, 3, 4, VIA3)
+    scatter(2, ACROSS, 1, 0, 1)
     scatter(2, ACROSS, 1, 0, 4)
-    scatter(0, HALF, 0, 2, 4, FAR)
-    scatter(0, OWN3, 0, 1, 0)
-    scatter(1, OWN1, 0, 3, 2)
-    scatter(0, OWN3, 0, 1, 1)
-    scatter(1, OWN1, 0, 3, 3)
-    scatter(1, OWN1, 0, 3, 4, VIA3)
+    scatter(0, OWN3, 0, 1, 3, HALF)
     scatter(1, OWN1, 0, 3, 0, HALF)
-    scatter(0, OWN3, 0, 1, 2, HALF)
-    scatter(1, OWN1, 0, 3, 1, HALF)
-    scatter(0, OWN3, 0, 1, 3, HALF)
+    scatter(0, OWN3, 0, 1, 5, HALF)
+    scatter(1, OWN1, 0, 3, 2, HALF)
     scatter(0, OWN3, 0, 1, 4, HALF, VIA1)
-    for p in (2, 3, 4, 0, 1):
-        total_ = sums(0, 0, p) + landed(ACROSS, p) + landed(OWN3, p) + landed(OWN1, p)
-        out[piece(p), :] = jnp.transpose(total_).astype(BF)
+    scatter(1, OWN1, 0, 3, 1, HALF, VIA3)
+    for p in PIECES:
+        total_ = sums(0, 0, p)
+        if p not in FOLD:
+            total_ = total_ + landed(ACROSS, p)
+        final[:, piece(p)] = total_
+    out_copies = []
+    for p in (3, 0, 5, 2, 4, 1):
+        total_ = final[:, piece(p)] + landed(OWN3, p) + landed(OWN1, p)
+        turned[piece(p), :] = jnp.transpose(total_).astype(BF)
+        copy = pltpu.make_async_copy(turned.at[piece(p)], out.at[piece(p)], out_sem.at[p])
+        copy.start()
+        out_copies.append(copy)
 
     for copy in sent:
         copy.wait_send()
@@ -453,6 +634,17 @@
 
     for i in range(3):
         weight_copy(i).wait_send()
+    for i in (0, 1):
+        fold_copy(i).wait_send()
+
+    @pl.when(core == 1 - yl)
+    def _():
+        for u in (0, 1):
+            for r in (0, 1):
+                far_first(r, u).wait_send()
+
+    for copy in out_copies:
+        copy.wait()
 
 
 def body(images, ctf_table, group_ids, projections, log_prior):
@@ -476,9 +668,17 @@
         pltpu.VMEM((2, 2, n_rows, PAD), BF),
         pltpu.VMEM((2, NX, n_rows, width), BF),
         pltpu.VMEM((9, n_rows, width), BF),
+        pltpu.VMEM((2, n_loc, width // 4), BF),
+        pltpu.VMEM((2, n_loc, width // 4), BF),
+        pltpu.VMEM((NZ, 2, n_loc, width // 4), BF),
+        pltpu.VMEM((2, n_rows, PAD), BF),
+        pltpu.VMEM((2, n_rows, SHARES[0] * width // 16), F32),
+        pltpu.VMEM((n_rows, width), F32),
+        pltpu.VMEM((width, n_rows), BF),
+        dma((len(SHARES),)),
         dma((4,)),
         dma((2,)),
-        dma((3, 12)),
+        dma((3, 15)),
         dma((2, NX, len(SHARES))),
         dma((2, NX)),
         dma((2, NX)),
@@ -491,6 +691,12 @@
         dma((3,)),
         dma((3, 13)),
         dma((9, len(SHARES))),
+        dma((2,)),
+        dma((3, 10)),
+        dma((2, NZ, 2)),
+        dma((2, 2)),
+        dma((2,)),
+        dma((2,)),
     ]
     vmem = pl.BlockSpec(memory_space=pltpu.VMEM)
     hbm = pl.BlockSpec(memory_space=pl.ANY)
@@ -498,7 +704,7 @@
         kernel,
         out_shape=jax.ShapeDtypeStruct((width, n_rows), BF),
         in_specs=[hbm, hbm, vmem, hbm, vmem],
-        out_specs=vmem,
+        out_specs=hbm,
         scratch_shapes=scratch,
         compiler_params=pltpu.CompilerParams(
             collective_id=0, has_side_effects=True, vmem_limit_bytes=56 << 20

time: 81.9 us -> 83.6 us (1.021)
  Pallas kernels: 79.9 us -> 81.6 us
    pallas_call x1, Pallas kernels: 79.9 us -> 81.6 us  [body(): pl.pallas_call(kernel, out_shape=jax.ShapeDtypeStruct((width, n_rows), BF...]
where the time goes in v3:
time: 83.6 us; the launch traced here: 83.5 us
  Pallas kernels  81.6 us (98%)
  local copies, waits for them, and re-layouts  1.87 us (2%)
    pallas_call x1, Pallas kernels, body(): pl.pallas_call(kernel, out_shape=jax.ShapeDtypeStruct((width, n_rows), BF...  81.6 us
    unnamed x1, local copies, waits for them, and re-layouts  1.87 us

profile of v3, /device:TPU:1, one launch (start us, length us, event | category | flops | bytes accessed | tf_op | source)
XLA Modules:
  0.0 83.5 jit_solution(9731497930045631919)
XLA Ops:
  0.0 81.6 %shard_map.55 = bf16[2048,128]{1,0:T(8,128)(2,1)} custom-call(bf16[176,32768]{1,0:T(8,128)(2,1)} %images.1, bf16[8,32768]{1,0:T(8,128)(2,1)} %ctf.1, s32[1,176]{1,0:T(1,128)} %bitcast.2, bf16[128,2048]{1,0:T(8,128)(2,1)} %proj.1, f32[1,128]{1,0:T(1,128)} %bitcast.3), custom_call_target="tpu_custom_call" | custom-call | tf_op jit(solution)/shard_map/pallas_call | solution.py:703
  81.6 1.9 %copy.7 = bf16[2048,128]{1,0:T(8,128)(2,1)} copy(bf16[2048,128]{1,0:T(8,128)(2,1)} %shard_map.55) | data formatting | bytes 1048576

commit v4 on v2

--- a/solution.py
+++ b/solution.py
@@ -60,6 +60,10 @@
     wts,
     part,
     rx,
+    begun,
+    final,
+    turned,
+    out_sem,
     raw_sem,
     loc_sem,
     g_send,
@@ -105,6 +109,14 @@
         yh_ = yh if s == 0 else 1 - yh
         return (yh_ * NX + lax.rem(x + j, NX)) * 2 + core_
 
+    barrier = pltpu.get_barrier_semaphore()
+    for who in (xp, xm, yp, sib, diag):
+        pl.semaphore_signal(barrier, inc=1, device_id=who, device_id_type=MESH)
+
+    @pl.loop(1, 2 * NZ)
+    def _(k):
+        pl.semaphore_signal(barrier, inc=1, device_id=peer(k), device_id_type=MESH)
+
     jobs = [(s, j, own) for s, j in ORDER for own in (0, 1)]
     n_raw = raw.shape[0]
 
@@ -122,14 +134,6 @@
         raw_copy(i).start()
     own_copy = pltpu.make_async_copy(proj, blocks.at[0, 0], loc_sem.at[0])
     own_copy.start()
-
-    barrier = pltpu.get_barrier_semaphore()
-    for who in (xp, xm, yp, sib, diag):
-        pl.semaphore_signal(barrier, inc=1, device_id=who, device_id_type=MESH)
-
-    @pl.loop(1, 2 * NZ)
-    def _(k):
-        pl.semaphore_signal(barrier, inc=1, device_id=peer(k), device_id_type=MESH)
 
     pl.semaphore_wait(barrier, 5 + 2 * NZ - 1)
 
@@ -340,8 +344,7 @@
             device_id_type=MESH,
         )
 
-    @pl.loop(1, 2 * NZ)
-    def _(k):
+    for k in sorted(range(1, 2 * NZ), key=lambda k: abs(k - NZ)):
         stat_copy(k).start()
 
     @pl.loop(1, 2 * NZ)
@@ -389,8 +392,11 @@
         ).wait_recv()
         return rx[kind, :, piece(p)].astype(F32)
 
-    def scatter(link, kind, s, j, p, *added):
-        total_ = sums(s, j, p)
+    def scatter(link, kind, s, j, p, *added, begun=None):
+        if begun is None:
+            total_ = sums(s, j, p)
+        else:
+            total_ = begun + nn(wts[s, 1, :, :n_loc], weighted[1, s, j, :, piece(p)])
         for k in added:
             total_ = total_ + landed(k, p)
         part[s, j, :, piece(p)] = total_.astype(BF)
@@ -406,12 +412,17 @@
         copy.start()
         sent.append(copy)
 
+    first = [(0, DIAG3, 1, 1, 0), (1, DIAG1, 1, 3, 0), (2, FAR, 1, 2, 0)]
+    for i, (_, _, s, j, p) in enumerate(first):
+        begun[i] = nn(wts[s, 0, :, :n_loc], weighted[0, s, j, :, piece(p)])
     weight_copy(0).wait_recv()
-    for a, p in zip(MIXED, PIECES):
-        scatter(2, FAR, 1, 2, a)
+    for i, job in enumerate(first):
+        scatter(*job, begun=begun[i])
+    for a, p in zip(MIXED[1:], PIECES[1:]):
         if p != VIA:
             scatter(0, DIAG3, 1, 1, p)
             scatter(1, DIAG1, 1, 3, p)
+        scatter(2, FAR, 1, 2, a)
     scatter(2, VIA3, 1, 3, VIA)
     scatter(2, VIA1, 1, 1, VIA)
     weight_copy(1).wait_recv()
@@ -436,9 +447,15 @@
     scatter(1, OWN1, 0, 3, 1, HALF)
     scatter(0, OWN3, 0, 1, 3, HALF)
     scatter(0, OWN3, 0, 1, 4, HALF, VIA1)
-    for p in (2, 3, 4, 0, 1):
-        total_ = sums(0, 0, p) + landed(ACROSS, p) + landed(OWN3, p) + landed(OWN1, p)
-        out[piece(p), :] = jnp.transpose(total_).astype(BF)
+    for p in PIECES:
+        final[:, piece(p)] = sums(0, 0, p) + landed(ACROSS, p)
+    out_copies = []
+    for p in (2, 0, 3, 1, 4):
+        total_ = final[:, piece(p)] + landed(OWN3, p) + landed(OWN1, p)
+        turned[piece(p), :] = jnp.transpose(total_).astype(BF)
+        copy = pltpu.make_async_copy(turned.at[piece(p)], out.at[piece(p)], out_sem.at[p])
+        copy.start()
+        out_copies.append(copy)
 
     for copy in sent:
         copy.wait_send()
@@ -453,6 +470,8 @@
 
     for i in range(3):
         weight_copy(i).wait_send()
+    for copy in out_copies:
+        copy.wait()
 
 
 def body(images, ctf_table, group_ids, projections, log_prior):
@@ -476,6 +495,10 @@
         pltpu.VMEM((2, 2, n_rows, PAD), BF),
         pltpu.VMEM((2, NX, n_rows, width), BF),
         pltpu.VMEM((9, n_rows, width), BF),
+        pltpu.VMEM((3, n_rows, SHARES[0] * width // 16), F32),
+        pltpu.VMEM((n_rows, width), F32),
+        pltpu.VMEM((width, n_rows), BF),
+        dma((len(SHARES),)),
         dma((4,)),
         dma((2,)),
         dma((3, 12)),
@@ -498,7 +521,7 @@
         kernel,
         out_shape=jax.ShapeDtypeStruct((width, n_rows), BF),
         in_specs=[hbm, hbm, vmem, hbm, vmem],
-        out_specs=vmem,
+        out_specs=hbm,
         scratch_shapes=scratch,
         compiler_params=pltpu.CompilerParams(
             collective_id=0, has_side_effects=True, vmem_limit_bytes=56 << 20

time: 81.9 us -> 81.6 us (level)
  no operation moved by 1% of the time
where the time goes in v4:
time: 81.6 us; the launch traced here: 81.4 us
  Pallas kernels  79.6 us (98%)
  local copies, waits for them, and re-layouts  1.87 us (2%)
    pallas_call x1, Pallas kernels, body(): pl.pallas_call(kernel, out_shape=jax.ShapeDtypeStruct((width, n_rows), BF...  79.6 us
    unnamed x1, local copies, waits for them, and re-layouts  1.87 us

profile of v4, /device:TPU:1, one launch (start us, length us, event | category | flops | bytes accessed | tf_op | source)
XLA Modules:
  0.0 81.4 jit_solution(15073029795831974523)
XLA Ops:
  0.0 79.6 %shard_map.55 = bf16[2048,128]{1,0:T(8,128)(2,1)} custom-call(bf16[176,32768]{1,0:T(8,128)(2,1)} %images.1, bf16[8,32768]{1,0:T(8,128)(2,1)} %ctf.1, s32[1,176]{1,0:T(1,128)} %bitcast.2, bf16[128,2048]{1,0:T(8,128)(2,1)} %proj.1, f32[1,128]{1,0:T(1,128)} %bitcast.3), custom_call_target="tpu_custom_call" | custom-call | tf_op jit(solution)/shard_map/pallas_call | solution.py:520
  79.6 1.9 %copy.7 = bf16[2048,128]{1,0:T(8,128)(2,1)} copy(bf16[2048,128]{1,0:T(8,128)(2,1)} %shard_map.55) | data formatting | bytes 1048576
